TPU v7x, 128 devices: a whole 4x4x4 slice. The times are simulated.
128 devices in a mesh: cfg: 2 (over core), seq: 32 (over y, z_lo, x), head: 2 (over z_hi).
Axes of the slice: x: 4, y: 4, z: 4 (z_hi: 2, z_lo: 2; z = z_hi * 2 + z_lo), core: 2. Of those that a mesh axis runs over, the one named last changes fastest.
Arguments:
- hidden: bfloat16 [2, 7168, 5120], P('cfg', 'seq', 'head'), may hold values from -6 to 6
- queries: bfloat16 [2, 7168, 2560], P('cfg', 'seq', 'head'), may hold values from -66 to 66
- keys: bfloat16 [2, 7168, 2560], P('cfg', 'seq', 'head'), may hold values from -12 to 12
- values: bfloat16 [2, 7168, 2560], P('cfg', 'seq', 'head'), may hold values from -6 to 6
- output_weight: bfloat16 [2560, 5120], P('head'), may hold values from -0.125 to 0.125
- adapter_down_weight: bfloat16 [8, 2560, 32], P(None, 'head'), may hold values from -0.125 to 0.125
- adapter_up_weight: bfloat16 [8, 32, 5120], P(None, None, 'head'), may hold values from -1 to 1
- request_adapters: int32 [4], replicated, may hold values from 0 to 7
- request_length: int32 [4], replicated, may hold values from 1 to 4480, 7168 in all
Outputs:
- guided: bfloat16 [7168, 5120], P('seq', 'head')
All inputs are finite; a program needn't handle non-finite values.
Results may differ from a plain program's by a relative error of at most 0.028.
Values may be sent and summed in bfloat16 or wider, within the bound.
A program may use at most 192 MiB of HBM per device.

v0:
```python
import functools
import math

import jax
import jax.numpy as jnp
from jax import lax
from jax.experimental import pallas as pl
from jax.experimental.pallas import tpu as pltpu
from jax.sharding import PartitionSpec as P

MESH = pl.DeviceIdType.MESH
HS = 128
GUIDE = 5.0
BK = 1536
PAIR = 2
PARTS = ((0, 64), (64, 48))
COLS = 512
ANY = pl.BlockSpec(memory_space=pl.ANY)
SMEM = pl.BlockSpec(memory_space=pltpu.SMEM)
VMEM = pl.BlockSpec(memory_space=pltpu.VMEM)


def place(head, branch):
    y = head // 2
    x = 2 * (head % 2) + (y + branch) % 2
    p = jnp.where(head < 8, y * 4 + x, jnp.where(head == 8, 1 - branch, 11 - branch))
    return (p // 4) * 8 + branch * 4 + p % 4


def role(s):
    x, y, branch = s % 4, s // 8, (s // 4) % 2
    p = y * 4 + x
    board = (x + y) % 2 == branch
    late = jnp.where(p == 1 - branch, 8, 9)
    active = jnp.logical_or(board, jnp.logical_or(p == 1 - branch, p == 11 - branch))
    return active, jnp.where(board, y * 2 + x // 2, late), branch


def signal(semaphore, *device):
    pl.semaphore_signal(semaphore, inc=1, device_id=device, device_id_type=MESH)


def scatter_kernel(
    q_ref, k_ref, v_ref, hid_ref, kbuf, vbuf, qbuf, hbuf,
    send_sem, kv_sem, q_sem, hid_sem, fwd_sem,
):
    b = lax.axis_index("cfg")
    s = lax.axis_index("seq")
    g = lax.axis_index("head")
    rows = q_ref.shape[1]
    heads = q_ref.shape[2] // HS
    half = hbuf.shape[0]
    active, _, branch = role(s)
    seqs = 32

    barrier = pltpu.get_barrier_semaphore()
    signal(barrier, 1 - b, s, g)

    @pl.when(active)
    def _():
        @pl.loop(0, seqs)
        def _(i):
            t = (s + i) % seqs

            @pl.when(jnp.logical_not(jnp.logical_and(t == s, branch == b)))
            def _():
                signal(barrier, branch, t, g)

    own = jnp.where(jnp.logical_and(active, branch == b), 1, 0)
    pl.semaphore_wait(barrier, 2 * heads + 1 - own)

    groups = kv_sem.shape[0]
    per = kbuf.shape[0] // groups

    other = pltpu.make_async_remote_copy(
        src_ref=hid_ref.at[0, pl.ds(pl.multiple_of((1 - b) * half, 16), half), :],
        dst_ref=hbuf,
        send_sem=hid_sem.at[0],
        recv_sem=hid_sem.at[1],
        device_id=(1 - b, s, g),
        device_id_type=MESH,
    )

    row0 = pl.multiple_of(s * rows, 32)
    qrow0 = pl.multiple_of((s // 2) * rows, 32)
    kind = (
        (k_ref, lambda: kbuf.at[pl.ds(row0, rows), :], kv_sem.at[s // (32 // groups)], 0),
        (v_ref, lambda: vbuf.at[pl.ds(row0, rows), :], kv_sem.at[s // (32 // groups)], 1),
        (q_ref, lambda: qbuf.at[pl.ds(qrow0, rows), :], q_sem, s % 2),
    )

    def each(i, act, kinds=(0, 1, 2)):
        h = (i + s) % heads
        target = place(h, b)
        for n in kinds:
            src, dst, sem, core = kind[n]
            piece = src.at[0, :, pl.ds(pl.multiple_of(h * HS, HS), HS)]
            mine = jnp.logical_and(target == s, core == b)
            act(n, piece, dst(), sem, core, target, mine, i)

    def start(n, piece, dst, sem, core, target, mine, i):
        @pl.when(mine)
        def _():
            pltpu.make_async_copy(piece, dst, sem).start()

        @pl.when(jnp.logical_not(mine))
        def _():
            pltpu.make_async_remote_copy(
                src_ref=piece, dst_ref=dst, send_sem=send_sem.at[i * 3 + n], recv_sem=sem,
                device_id=(core, target, g), device_id_type=MESH,
            ).start()

    def finish(n, piece, dst, sem, core, target, mine, i):
        @pl.when(jnp.logical_not(mine))
        def _():
            pltpu.make_async_remote_copy(
                src_ref=piece, dst_ref=dst, send_sem=send_sem.at[i * 3 + n], recv_sem=sem,
                device_id=(core, target, g), device_id_type=MESH,
            ).wait_send()

    for n in range(3):

        @pl.loop(0, heads)
        def _(i):
            each(i, start, (n,))

    other.start()

    def forward(buf, n):
        part = buf.at[pl.ds(n * per, per), :]
        return pltpu.make_async_remote_copy(
            src_ref=part, dst_ref=part, send_sem=fwd_sem.at[0, n], recv_sem=fwd_sem.at[1, n],
            device_id=(1 - b, s, g), device_id_type=MESH,
        )

    def landed(buf, sem):
        pltpu.make_async_copy(buf, buf, sem).wait()

    for core, (got, came) in enumerate(((kbuf, vbuf), (vbuf, kbuf))):

        @pl.when(jnp.logical_and(active, b == core))
        def _():
            for n in range(groups):
                landed(got.at[pl.ds(n * per, per), :], kv_sem.at[n])
                forward(got, n).start()
            for n in range(groups):
                forward(got, n).wait_send()
                forward(came, n).wait_recv()
            landed(qbuf, q_sem)

    @pl.loop(0, heads)
    def _(i):
        each(i, finish)

    other.wait()


def attention_kernel(len_ref, q_ref, k_ref, v_ref, o_ref, s_ref, m_ref, acc_ref):
    c = lax.axis_index("cfg")
    s = lax.axis_index("seq")
    active, _, _ = role(s)
    rows = acc_ref.shape[0]
    piece = rows // PAIR
    tokens = k_ref.shape[0]
    factor = math.log2(math.e) / math.sqrt(HS)
    e0 = len_ref[0]
    e1 = e0 + len_ref[1]
    e2 = e1 + len_ref[2]

    def segment(pos):
        return (
            (pos >= e0).astype(jnp.int32)
            + (pos >= e1).astype(jnp.int32)
            + (pos >= e2).astype(jnp.int32)
        )

    @pl.loop(0, jnp.where(active, q_ref.shape[0] // rows, 0))
    def _(tile):
        first = (2 * PAIR * tile + c) * piece
        last = first + (2 * PAIR - 1) * piece - 1
        own = pl.ds(pl.multiple_of(tile * rows, 32), rows)
        seg_first = segment(first)
        seg_last = segment(last)
        starts = (0, e0, e1, e2)
        ends = (e0, e1, e2, tokens)
        lo = jnp.int32(0)
        hi = jnp.int32(tokens)
        for n in range(4):
            lo = jnp.where(seg_first == n, starts[n], lo)
            hi = jnp.where(seg_last == n, ends[n], hi)
        base = (lo // 32) * 32
        blocks = pl.cdiv(hi - base, BK)
        single = seg_first == seg_last
        row = lax.broadcasted_iota(jnp.int32, (rows, 1), 0)
        seg_q = segment(first + row + (row // piece) * piece)
        m_ref[...] = jnp.full_like(m_ref, -1e30)

        def widest(x):
            out = m_ref[...]
            for n in range(BK // HS):
                out = jnp.maximum(out, x[:, n * HS : (n + 1) * HS])
            m_ref[...] = out

        def scores(at):
            return lax.dot_general(
                q_ref[own, :], k_ref[pl.ds(at, BK), :], (((1,), (1,)), ((), ())),
                preferred_element_type=jnp.float32,
            )

        @pl.loop(0, blocks)
        def _(n):
            logical = base + n * BK
            at = pl.multiple_of(jnp.minimum(logical, tokens - BK), 32)
            whole = jnp.logical_and(
                single, jnp.logical_and(logical >= lo, logical + BK <= hi)
            )

            @pl.when(whole)
            def _():
                score = scores(at)
                s_ref[n] = score
                widest(score)

            @pl.when(jnp.logical_not(whole))
            def _():
                pos = at + lax.broadcasted_iota(jnp.int32, (1, BK), 1)
                seg_k = jnp.where(pos >= logical, segment(pos), -1)
                score = jnp.where(seg_q == seg_k, scores(at), -jnp.inf)
                s_ref[n] = score
                widest(score)

        m_ref[...] = jnp.broadcast_to(
            jnp.max(m_ref[...], axis=1, keepdims=True), m_ref.shape
        )
        acc_ref[...] = jnp.zeros_like(acc_ref)

        @pl.loop(0, blocks)
        def _(n):
            at = pl.multiple_of(jnp.minimum(base + n * BK, tokens - BK), 32)
            top = m_ref[...]
            weight = jnp.concatenate(
                [
                    jnp.exp2((s_ref[n, :, j * HS : (j + 1) * HS] - top) * factor).astype(
                        jnp.bfloat16
                    )
                    for j in range(BK // HS)
                ],
                axis=1,
            )
            values = jnp.concatenate(
                [v_ref[pl.ds(at, BK), :], jnp.ones((BK, HS), jnp.bfloat16)], axis=1
            )
            acc_ref[...] += jnp.dot(weight, values, preferred_element_type=jnp.float32)

        o_ref[own, :] = (acc_ref[:, :HS] / acc_ref[:, HS:]).astype(o_ref.dtype)


def project_kernel(
    len_ref, ad_ref, o_ref, hid_ref, hbuf, w_ref, down_ref, up_ref, out_ref,
    att, wo, wm, downv, upv, hm, ho, dv, inner, picked, pm, psend, precv, isend, irecv, outv,
    load_sem, o_send, o_sem, p_sem, i_sem, out_sem,
):
    b = lax.axis_index("cfg")
    s = lax.axis_index("seq")
    g = lax.axis_index("head")
    active, head, branch = role(s)
    half, width = outv.shape
    rows = 2 * half
    heads = att.shape[2] // HS
    blocks = o_ref.shape[0] // rows
    chunks = range(width // COLS)
    top = pl.multiple_of(b * half, 16)

    barrier = pltpu.get_barrier_semaphore()
    signal(barrier, 1 - b, s, g)
    signal(barrier, b, s, 1 - g)

    for origin in range(2):

        @pl.loop(0, heads)
        def _(i):
            t = place((i + s) % heads, origin)

            @pl.when(jnp.logical_not(jnp.logical_and(t == s, s % 2 == b)))
            def _():
                signal(barrier, s % 2, t, g)

    own = jnp.where(s % 2 == b, 1, 0)
    pl.semaphore_wait(barrier, 2 + jnp.where(active, 2 * blocks - own, 0))

    def send_o(i, n, core, go):
        j = 2 * i + b
        first, count = PARTS[n]
        piece = o_ref.at[pl.ds(pl.multiple_of(i * rows + core * half + first, 16), count), :]
        dst = att.at[branch, pl.ds(first, count), pl.ds(pl.multiple_of(head * HS, HS), HS)]
        here = jnp.logical_and(j == s, core == b)

        @pl.when(here)
        def _():
            if go:
                pltpu.make_async_copy(piece, dst, o_sem.at[n]).start()

        @pl.when(jnp.logical_not(here))
        def _():
            copy = pltpu.make_async_remote_copy(
                src_ref=piece, dst_ref=dst, send_sem=o_send.at[n, core, i], recv_sem=o_sem.at[n],
                device_id=(core, j, g), device_id_type=MESH,
            )
            if go:
                copy.start()
            else:
                copy.wait_send()

    @pl.when(active)
    def _():
        for n in range(len(PARTS)):

            @pl.loop(0, blocks)
            def _(i):
                for core in range(2):
                    send_o((i + s // 2) % blocks, n, core, True)

    loads = [
        (down_ref, downv),
        (w_ref.at[:, pl.ds(pl.multiple_of((1 - g) * width, width), width)], wo),
        (w_ref.at[:, pl.ds(pl.multiple_of(g * width, width), width)], wm),
        (up_ref, upv),
        (hid_ref.at[0, pl.ds(top, half), :], hm),
        (hbuf, ho),
    ]
    loads = [pltpu.make_async_copy(a, z, load_sem.at[n]) for n, (a, z) in enumerate(loads)]
    for copy in loads:
        copy.start()

    def partner(src, dst, sems):
        return pltpu.make_async_remote_copy(
            src_ref=src, dst_ref=dst, send_sem=sems.at[0], recv_sem=sems.at[1],
            device_id=(b, s, 1 - g), device_id_type=MESH,
        )

    rank = downv.shape[0] // 8
    pos = s * rows + b * half + lax.broadcasted_iota(jnp.int32, picked.shape, 0)
    lane = lax.broadcasted_iota(jnp.int32, picked.shape, 1)
    e0 = len_ref[0]
    e1 = e0 + len_ref[1]
    e2 = e1 + len_ref[2]
    adapter = jnp.where(
        pos < e1,
        jnp.where(pos < e0, ad_ref[0], ad_ref[1]),
        jnp.where(pos < e2, ad_ref[2], ad_ref[3]),
    )
    picked[...] = ((lane // rank) == adapter).astype(jnp.float32)
    for copy in loads:
        copy.wait()
    scale_m = jnp.where(b == 0, GUIDE, 1.0 - GUIDE).astype(jnp.float32)
    scale_o = jnp.where(b == 0, 1.0 - GUIDE, GUIDE).astype(jnp.float32)
    pm[...] = scale_m * hm[...].astype(jnp.float32) + scale_o * ho[...].astype(jnp.float32)

    def column(c):
        return slice(c * COLS, (c + 1) * COLS)

    for n, (first, count) in enumerate(PARTS):
        sl = slice(first, first + count)
        came = att.at[:, pl.ds(first, count), :]
        pltpu.make_async_copy(came, came, o_sem.at[n]).wait()
        dv[sl, :] = (
            GUIDE * att[0, sl, :].astype(jnp.float32)
            + (1.0 - GUIDE) * att[1, sl, :].astype(jnp.float32)
        ).astype(jnp.bfloat16)
        for c in chunks:
            psend[c, sl, :] = jnp.dot(
                dv[sl, :], wo[:, column(c)], preferred_element_type=jnp.float32
            ).astype(jnp.bfloat16)
            partner(psend.at[c, sl, :], precv.at[c, sl, :], p_sem.at[n, c]).start()
            if c == 0:
                inner[sl, :] = (
                    lax.dot_general(
                        dv[sl, :], downv[...], (((1,), (1,)), ((), ())),
                        preferred_element_type=jnp.float32,
                    )
                    * picked[sl, :]
                )
                isend[sl, :] = inner[sl, :].astype(jnp.bfloat16)
                partner(isend.at[sl, :], irecv.at[sl, :], i_sem.at[n]).start()
    for c in chunks:
        pm[:, column(c)] += jnp.dot(
            dv[...], wm[:, column(c)], preferred_element_type=jnp.float32
        )
    for n, (first, count) in enumerate(PARTS):
        sl = slice(first, first + count)
        partner(isend.at[sl, :], irecv.at[sl, :], i_sem.at[n]).wait()
    both = (inner[...] + irecv[...].astype(jnp.float32)).astype(jnp.bfloat16)
    for c in chunks:
        pm[:, column(c)] += jnp.dot(both, upv[:, column(c)], preferred_element_type=jnp.float32)
    last = []
    for n, (first, count) in enumerate(PARTS):
        sl = slice(first, first + count)
        for c in chunks:
            partner(psend.at[c, sl, :], precv.at[c, sl, :], p_sem.at[n, c]).wait()
            outv[sl, column(c)] = (
                pm[sl, column(c)] + precv[c, sl, :].astype(jnp.float32)
            ).astype(jnp.bfloat16)
            piece = outv.at[sl, pl.ds(c * COLS, COLS)]
            result = out_ref.at[pl.ds(pl.multiple_of(top + first, 16), count), pl.ds(c * COLS, COLS)]
            last.append(
                pltpu.make_async_remote_copy(
                    src_ref=piece, dst_ref=result,
                    send_sem=out_sem.at[n, c, 0], recv_sem=out_sem.at[n, c, 1],
                    device_id=(1 - b, s, g), device_id_type=MESH,
                )
            )
            last.append(pltpu.make_async_copy(piece, result, out_sem.at[n, c, 2]))
            last[-2].start()
            last[-1].start()

    @pl.when(active)
    def _():
        for n in range(len(PARTS)):

            @pl.loop(0, blocks)
            def _(i):
                for core in range(2):
                    send_o(i, n, core, False)

    for copy in last:
        copy.wait()


def local(
    hidden, queries, keys, values, output_weight, adapter_down_weight, adapter_up_weight,
    request_adapters, request_length,
):
    rows, width = queries.shape[1:]
    tokens = rows * 32
    bf16, f32 = jnp.bfloat16, jnp.float32
    dma = pltpu.SemaphoreType.DMA
    down = adapter_down_weight.transpose(0, 2, 1).reshape(-1, width)
    up = adapter_up_weight.reshape(-1, adapter_up_weight.shape[2])
    rank = up.shape[0]

    kbuf, vbuf, qbuf, hbuf = pl.pallas_call(
        scatter_kernel,
        out_shape=(
            jax.ShapeDtypeStruct((tokens, HS), bf16),
            jax.ShapeDtypeStruct((tokens, HS), bf16),
            jax.ShapeDtypeStruct((tokens // 2, HS), bf16),
            jax.ShapeDtypeStruct((rows // 2, 2 * width), bf16),
        ),
        in_specs=[ANY] * 4,
        out_specs=(ANY,) * 4,
        scratch_shapes=[dma((30,)), dma((4,)), dma, dma((2,)), dma((2, 4))],
        compiler_params=pltpu.CompilerParams(
            has_side_effects=True, collective_id=1, vmem_limit_bytes=2**20
        ),
        name="scatter_heads",
    )(queries, keys, values, hidden)

    steps = tokens // 2 // rows
    tile = PAIR * rows
    o = pl.pallas_call(
        attention_kernel,
        out_shape=jax.ShapeDtypeStruct((tokens // 2, HS), bf16),
        in_specs=[SMEM, VMEM, VMEM, VMEM],
        out_specs=VMEM,
        scratch_shapes=[
            pltpu.VMEM((pl.cdiv(tokens, BK), tile, BK), f32),
            pltpu.VMEM((tile, HS), f32),
            pltpu.VMEM((tile, 2 * HS), f32),
        ],
        compiler_params=pltpu.CompilerParams(vmem_limit_bytes=40 * 2**20),
        name="attend",
    )(request_length, qbuf, kbuf, vbuf)

    half = rows // 2
    chunks = 2 * width // COLS
    parts = len(PARTS)
    return pl.pallas_call(
        project_kernel,
        out_shape=jax.ShapeDtypeStruct((rows, 2 * width), bf16),
        in_specs=[SMEM, SMEM] + [ANY] * 6,
        out_specs=ANY,
        scratch_shapes=[
            pltpu.VMEM((2, half, width), bf16),
            pltpu.VMEM((width, 2 * width), bf16),
            pltpu.VMEM((width, 2 * width), bf16),
            pltpu.VMEM((rank, width), bf16),
            pltpu.VMEM((rank, 2 * width), bf16),
            pltpu.VMEM((half, 2 * width), bf16),
            pltpu.VMEM((half, 2 * width), bf16),
            pltpu.VMEM((half, width), bf16),
            pltpu.VMEM((half, rank), f32),
            pltpu.VMEM((half, rank), f32),
            pltpu.VMEM((half, 2 * width), f32),
            pltpu.VMEM((chunks, half, COLS), bf16),
            pltpu.VMEM((chunks, half, COLS), bf16),
            pltpu.VMEM((half, rank), bf16),
            pltpu.VMEM((half, rank), bf16),
            pltpu.VMEM((half, 2 * width), bf16),
            dma((6,)), dma((parts, 2, steps)), dma((parts,)),
            dma((parts, chunks, 2)), dma((parts, 2)), dma((parts, chunks, 3)),
        ],
        compiler_params=pltpu.CompilerParams(
            has_side_effects=True, collective_id=2, vmem_limit_bytes=48 * 2**20
        ),
        name="project",
    )(request_length, request_adapters, o, hidden, hbuf, output_weight, down, up)


def solution(mesh):
    return jax.shard_map(
        local,
        mesh=mesh,
        in_specs=(
            P("cfg", "seq", "head"),
            P("cfg", "seq", "head"),
            P("cfg", "seq", "head"),
            P("cfg", "seq", "head"),
            P("head", None),
            P(None, "head", None),
            P(None, None, "head"),
            P(),
            P(),
        ),
        out_specs=P("seq", "head"),
        check_vma=False,
    )
```

profile of v0, /device:TPU:1, one launch (start us, length us, event | category | flops | bytes accessed | tf_op | source)
XLA Modules:
  0.0 105.7 jit_solution(10234982089133891117)
XLA Ops:
  0.0 0.0 copy-start
  0.0 1.3 %copy-done = bf16[1,224,2560]{2,1,0:T(8,128)(2,1)S(1)} copy-done((bf16[1,224,2560]{2,1,0:T(8,128)(2,1)S(1)}, bf16[1,224,2560]{2,1,0:T(8,128)(2,1)}, u32[]{:S(2)}) %copy-start) | copy-done | bytes 1146904
  1.3 0.0 copy-start.4
  1.3 1.1 copy-done.4
  2.3 0.0 copy-start.5
  2.3 1.1 copy-done.5
  3.4 0.0 copy-start.6
  3.4 1.1 copy-done.6
  4.4 0.0 copy-start.7
  4.4 42.0 %scatter_heads.1 = (bf16[7168,128]{1,0:T(8,128)(2,1)S(1)}, bf16[7168,128]{1,0:T(8,128)(2,1)S(1)}, bf16[3584,128]{1,0:T(8,128)(2,1)S(1)}, bf16[112,2560]{1,0:T(8,128)(2,1)S(1)}) custom-call(bf16[1,224,1280]{2,1,0:T(8,128)(2,1)S(1)} %copy-done.4, bf16[1,224,1280]{2,1,0:T(8,128)(2,1)S(1)} %copy-done.5, bf16[1,224,1280]{2,1,0:T(8,128)(2,1)S(1)} %copy-done.6, ...), custom_call_target="tpu_custom_call" | custom-call | tf_op jit(solution)/shard_map/scatter_heads/pallas_call | solution.py:441
  46.4 0.0 copy-done.7
  46.4 0.0 copy-start.1
  46.4 0.0 copy-start.2
  46.5 0.0 copy-start.3
  46.5 0.0 copy-start.8
  46.5 23.8 %attend.1.o_ref = bf16[3584,128]{1,0:T(8,128)(2,1)S(1)} custom-call(s32[4]{0:T(128)S(1)} %copy-done.7, bf16[3584,128]{1,0:T(8,128)(2,1)S(1)} %get-tuple-element.9.q_ref, bf16[7168,128]{1,0:T(8,128)(2,1)S(1)} %get-tuple-element.10.k_ref, bf16[7168,128]{1,0:T(8,128)(2,1)S(1)} %get-tuple-element.11.v_ref), custom_call_target="tpu_custom_call" | custom-call | tf_op jit(solution)/shard_map/attend/pallas_call | solution.py:460
  70.3 0.0 copy-done.1
  70.3 0.0 copy-done.2
  70.4 0.0 copy-done.3
  70.4 0.0 copy-done.8
  70.4 34.3 %project.1 = bf16[224,2560]{1,0:T(8,128)(2,1)S(1)} custom-call(s32[4]{0:T(128)S(1)} %copy-done.7, s32[4]{0:T(128)S(1)} %copy-done.8, bf16[3584,128]{1,0:T(8,128)(2,1)S(1)} %attend.1.o_ref, bf16[1,224,2560]{2,1,0:T(8,128)(2,1)S(1)} %copy-done.1, bf16[112,2560]{1,0:T(8,128)(2,1)S(1)} %get-tuple-element.12.hbuf, bf16[1280,5120]{1,0:T(8,128)(2,1)} %w_ref.1, ...), custom_call_target="tpu_custom_call" | custom-call | tf_op jit(solution)/shard_map/project/pallas_call | solution.py:477
  104.7 1.0 copy.11
Async XLA Ops:
  0.0 1.3 %copy-start = (bf16[1,224,2560]{2,1,0:T(8,128)(2,1)S(1)}, bf16[1,224,2560]{2,1,0:T(8,128)(2,1)}, u32[]{:S(2)}) copy-start(bf16[1,224,2560]{2,1,0:T(8,128)(2,1)} %hid_ref.3) | copy-start | bytes 3440644
  1.3 1.1 %copy-start.4 = (bf16[1,224,1280]{2,1,0:T(8,128)(2,1)S(1)}, bf16[1,224,1280]{2,1,0:T(8,128)(2,1)}, u32[]{:S(2)}) copy-start(bf16[1,224,1280]{2,1,0:T(8,128)(2,1)} %q_ref.1) | copy-start | bytes 1720324
  2.3 1.1 %copy-start.5 = (bf16[1,224,1280]{2,1,0:T(8,128)(2,1)S(1)}, bf16[1,224,1280]{2,1,0:T(8,128)(2,1)}, u32[]{:S(2)}) copy-start(bf16[1,224,1280]{2,1,0:T(8,128)(2,1)} %k_ref.1) | copy-start | bytes 1720324
  3.4 1.1 %copy-start.6 = (bf16[1,224,1280]{2,1,0:T(8,128)(2,1)S(1)}, bf16[1,224,1280]{2,1,0:T(8,128)(2,1)}, u32[]{:S(2)}) copy-start(bf16[1,224,1280]{2,1,0:T(8,128)(2,1)} %v_ref.1) | copy-start | bytes 1720324
  4.4 42.0 %copy-start.7 = (s32[4]{0:T(128)S(1)}, s32[4]{0:T(128)}, u32[]{:S(2)}) copy-start(s32[4]{0:T(128)} %len_ref.3) | copy-start | bytes 52
  46.4 23.9 %copy-start.1 = (bf16[1,224,2560]{2,1,0:T(8,128)(2,1)S(1)}, bf16[1,224,2560]{2,1,0:T(8,128)(2,1)}, u32[]{:S(2)}) copy-start(bf16[1,224,2560]{2,1,0:T(8,128)(2,1)} %hid_ref.3) | copy-start | bytes 3440644
  46.4 23.9 %copy-start.2 = (bf16[8,32,2560]{2,1,0:T(8,128)(2,1)S(1)}, bf16[8,32,2560]{2,1,0:T(8,128)(2,1)}, u32[]{:S(2)}) copy-start(bf16[8,32,2560]{2,1,0:T(8,128)(2,1)} %param.15) | copy-start | bytes 3932164
  46.5 23.9 %copy-start.3 = (bf16[8,1280,32]{1,2,0:T(8,128)(2,1)S(1)}, bf16[8,1280,32]{1,2,0:T(8,128)(2,1)}, u32[]{:S(2)}) copy-start(bf16[8,1280,32]{1,2,0:T(8,128)(2,1)} %param.14) | copy-start | bytes 1966084
  46.5 23.9 %copy-start.8 = (s32[4]{0:T(128)S(1)}, s32[4]{0:T(128)}, u32[]{:S(2)}) copy-start(s32[4]{0:T(128)} %ad_ref.1) | copy-start | bytes 52
where the time goes:
time: 106 us
  Pallas kernels  100 us (94%)
  local copies, waits for them, and re-layouts  5.47 us (5%)
    pallas_call x1, Pallas kernels, local(): pl.pallas_call(scatter_kernel, out_shape=(jax.ShapeDtypeStruct((tokens, H...  42 us
    pallas_call x1, Pallas kernels, local(): pl.pallas_call(project_kernel, out_shape=jax.ShapeDtypeStruct((rows, 2 *...  34.3 us
    pallas_call x1, Pallas kernels, local(): pl.pallas_call(attention_kernel, out_shape=jax.ShapeDtypeStruct((tokens /...  23.8 us
    unnamed x19, local copies, waits for them, and re-layouts  5.47 us

commit v1 on v0

--- a/solution.py
+++ b/solution.py
@@ -453,7 +453,7 @@
             has_side_effects=True, collective_id=1, vmem_limit_bytes=2**20
         ),
         name="scatter_heads",
-    )(queries, keys, values, hidden)
+    )(*(pltpu.with_memory_space_constraint(x, pltpu.HBM) for x in (queries, keys, values, hidden)))
 
     steps = tokens // 2 // rows
     tile = PAIR * rows

time: 106 us -> 102 us (0.962)
  local copies, waits for them, and re-layouts: 5.47 us -> 1.03 us
    unnamed x19 -> x11, local copies, waits for them, and re-layouts: 5.47 us -> 1.03 us
where the time goes in v1:
time: 102 us
  Pallas kernels  100 us (98%)
  local copies, waits for them, and re-layouts  1.03 us (1%)
    pallas_call x1, Pallas kernels, local(): pl.pallas_call(scatter_kernel, out_shape=(jax.ShapeDtypeStruct((tokens, H...  42.3 us
    pallas_call x1, Pallas kernels, local(): pl.pallas_call(project_kernel, out_shape=jax.ShapeDtypeStruct((rows, 2 *...  34.3 us
    pallas_call x1, Pallas kernels, local(): pl.pallas_call(attention_kernel, out_shape=jax.ShapeDtypeStruct((tokens /...  23.8 us

profile of v1, /device:TPU:1, one launch (start us, length us, event | category | flops | bytes accessed | tf_op | source)
XLA Modules:
  0.0 101.6 jit_solution(10969230038981803579)
XLA Ops:
  0.0 0.0 copy-start.3
  0.0 42.3 %scatter_heads.1 = (bf16[7168,128]{1,0:T(8,128)(2,1)S(1)}, bf16[7168,128]{1,0:T(8,128)(2,1)S(1)}, bf16[3584,128]{1,0:T(8,128)(2,1)S(1)}, bf16[112,2560]{1,0:T(8,128)(2,1)S(1)}) custom-call(bf16[1,224,1280]{2,1,0:T(8,128)(2,1)} %q_ref.1, bf16[1,224,1280]{2,1,0:T(8,128)(2,1)} %k_ref.1, bf16[1,224,1280]{2,1,0:T(8,128)(2,1)} %v_ref.1, bf16[1,224,2560]{2,1,0:T(8,128)(2,1)} %hid_ref.3), custom_call_target="tpu_custom_call" | custom-call | tf_op jit(solution)/shard_map/scatter_heads/pallas_call | solution.py:441
  42.3 0.0 copy-done.3
  42.3 0.0 copy-start
  42.3 0.0 copy-start.1
  42.3 0.0 copy-start.2
  42.3 0.0 copy-start.4
  42.3 23.8 %attend.1.o_ref = bf16[3584,128]{1,0:T(8,128)(2,1)S(1)} custom-call(s32[4]{0:T(128)S(1)} %copy-done.3, bf16[3584,128]{1,0:T(8,128)(2,1)S(1)} %get-tuple-element.9.q_ref, bf16[7168,128]{1,0:T(8,128)(2,1)S(1)} %get-tuple-element.10.k_ref, bf16[7168,128]{1,0:T(8,128)(2,1)S(1)} %get-tuple-element.11.v_ref), custom_call_target="tpu_custom_call" | custom-call | tf_op jit(solution)/shard_map/attend/pallas_call | solution.py:460
  66.2 0.0 copy-done
  66.2 0.0 copy-done.1
  66.2 0.0 copy-done.2
  66.2 0.0 copy-done.4
  66.2 34.3 %project.1 = bf16[224,2560]{1,0:T(8,128)(2,1)S(1)} custom-call(s32[4]{0:T(128)S(1)} %copy-done.3, s32[4]{0:T(128)S(1)} %copy-done.4, bf16[3584,128]{1,0:T(8,128)(2,1)S(1)} %attend.1.o_ref, bf16[1,224,2560]{2,1,0:T(8,128)(2,1)S(1)} %copy-done, bf16[112,2560]{1,0:T(8,128)(2,1)S(1)} %get-tuple-element.12.hbuf, bf16[1280,5120]{1,0:T(8,128)(2,1)} %w_ref.1, ...), custom_call_target="tpu_custom_call" | custom-call | tf_op jit(solution)/shard_map/project/pallas_call | solution.py:477
  100.6 1.0 copy.11
Async XLA Ops:
  0.0 42.3 %copy-start.3 = (s32[4]{0:T(128)S(1)}, s32[4]{0:T(128)}, u32[]{:S(2)}) copy-start(s32[4]{0:T(128)} %len_ref.3) | copy-start | bytes 52
  42.3 23.9 %copy-start = (bf16[1,224,2560]{2,1,0:T(8,128)(2,1)S(1)}, bf16[1,224,2560]{2,1,0:T(8,128)(2,1)}, u32[]{:S(2)}) copy-start(bf16[1,224,2560]{2,1,0:T(8,128)(2,1)} %hid_ref.3) | copy-start | bytes 3440644
  42.3 23.9 %copy-start.1 = (bf16[8,32,2560]{2,1,0:T(8,128)(2,1)S(1)}, bf16[8,32,2560]{2,1,0:T(8,128)(2,1)}, u32[]{:S(2)}) copy-start(bf16[8,32,2560]{2,1,0:T(8,128)(2,1)} %param.15) | copy-start | bytes 3932164
  42.3 23.9 %copy-start.2 = (bf16[8,1280,32]{1,2,0:T(8,128)(2,1)S(1)}, bf16[8,1280,32]{1,2,0:T(8,128)(2,1)}, u32[]{:S(2)}) copy-start(bf16[8,1280,32]{1,2,0:T(8,128)(2,1)} %param.14) | copy-start | bytes 1966084
  42.3 23.9 %copy-start.4 = (s32[4]{0:T(128)S(1)}, s32[4]{0:T(128)}, u32[]{:S(2)}) copy-start(s32[4]{0:T(128)} %ad_ref.1) | copy-start | bytes 52

commit v2 on v1

--- a/solution.py
+++ b/solution.py
@@ -155,7 +155,9 @@
     other.wait()
 
 
-def attention_kernel(len_ref, q_ref, k_ref, v_ref, o_ref, s_ref, m_ref, acc_ref):
+def attention_kernel(
+    len_ref, q_ref, k_ref, v_ref, w_ref, o_ref, kept_ref, s_ref, m_ref, acc_ref, w_sem
+):
     c = lax.axis_index("cfg")
     s = lax.axis_index("seq")
     active, _, _ = role(s)
@@ -163,6 +165,8 @@
     piece = rows // PAIR
     tokens = k_ref.shape[0]
     factor = math.log2(math.e) / math.sqrt(HS)
+    fetch = pltpu.make_async_copy(w_ref, kept_ref, w_sem)
+    fetch.start()
     e0 = len_ref[0]
     e1 = e0 + len_ref[1]
     e2 = e1 + len_ref[2]
@@ -254,11 +258,13 @@
 
         o_ref[own, :] = (acc_ref[:, :HS] / acc_ref[:, HS:]).astype(o_ref.dtype)
 
+    fetch.wait()
+
 
 def project_kernel(
     len_ref, ad_ref, o_ref, hid_ref, hbuf, w_ref, down_ref, up_ref, out_ref,
-    att, wo, wm, downv, upv, hm, ho, dv, inner, picked, pm, psend, precv, isend, irecv, outv,
-    load_sem, o_send, o_sem, p_sem, i_sem, out_sem,
+    att, dv, inner, picked, pm, psend, precv, isend, irecv, outv,
+    o_send, o_sem, p_sem, i_sem, out_sem,
 ):
     b = lax.axis_index("cfg")
     s = lax.axis_index("seq")
@@ -320,25 +326,13 @@
                 for core in range(2):
                     send_o((i + s // 2) % blocks, n, core, True)
 
-    loads = [
-        (down_ref, downv),
-        (w_ref.at[:, pl.ds(pl.multiple_of((1 - g) * width, width), width)], wo),
-        (w_ref.at[:, pl.ds(pl.multiple_of(g * width, width), width)], wm),
-        (up_ref, upv),
-        (hid_ref.at[0, pl.ds(top, half), :], hm),
-        (hbuf, ho),
-    ]
-    loads = [pltpu.make_async_copy(a, z, load_sem.at[n]) for n, (a, z) in enumerate(loads)]
-    for copy in loads:
-        copy.start()
-
     def partner(src, dst, sems):
         return pltpu.make_async_remote_copy(
             src_ref=src, dst_ref=dst, send_sem=sems.at[0], recv_sem=sems.at[1],
             device_id=(b, s, 1 - g), device_id_type=MESH,
         )
 
-    rank = downv.shape[0] // 8
+    rank = down_ref.shape[0] // 8
     pos = s * rows + b * half + lax.broadcasted_iota(jnp.int32, picked.shape, 0)
     lane = lax.broadcasted_iota(jnp.int32, picked.shape, 1)
     e0 = len_ref[0]
@@ -350,14 +344,16 @@
         jnp.where(pos < e2, ad_ref[2], ad_ref[3]),
     )
     picked[...] = ((lane // rank) == adapter).astype(jnp.float32)
-    for copy in loads:
-        copy.wait()
     scale_m = jnp.where(b == 0, GUIDE, 1.0 - GUIDE).astype(jnp.float32)
     scale_o = jnp.where(b == 0, 1.0 - GUIDE, GUIDE).astype(jnp.float32)
-    pm[...] = scale_m * hm[...].astype(jnp.float32) + scale_o * ho[...].astype(jnp.float32)
+    hm = hid_ref[0, pl.ds(top, half), :].astype(jnp.float32)
+    pm[...] = scale_m * hm + scale_o * hbuf[...].astype(jnp.float32)
 
     def column(c):
         return slice(c * COLS, (c + 1) * COLS)
+
+    def weight(side, c):
+        return w_ref[:, pl.ds(pl.multiple_of(side * width + c * COLS, COLS), COLS)]
 
     for n, (first, count) in enumerate(PARTS):
         sl = slice(first, first + count)
@@ -369,13 +365,13 @@
         ).astype(jnp.bfloat16)
         for c in chunks:
             psend[c, sl, :] = jnp.dot(
-                dv[sl, :], wo[:, column(c)], preferred_element_type=jnp.float32
+                dv[sl, :], weight(1 - g, c), preferred_element_type=jnp.float32
             ).astype(jnp.bfloat16)
             partner(psend.at[c, sl, :], precv.at[c, sl, :], p_sem.at[n, c]).start()
             if c == 0:
                 inner[sl, :] = (
                     lax.dot_general(
-                        dv[sl, :], downv[...], (((1,), (1,)), ((), ())),
+                        dv[sl, :], down_ref[...], (((1,), (1,)), ((), ())),
                         preferred_element_type=jnp.float32,
                     )
                     * picked[sl, :]
@@ -384,14 +380,14 @@
                 partner(isend.at[sl, :], irecv.at[sl, :], i_sem.at[n]).start()
     for c in chunks:
         pm[:, column(c)] += jnp.dot(
-            dv[...], wm[:, column(c)], preferred_element_type=jnp.float32
+            dv[...], weight(g, c), preferred_element_type=jnp.float32
         )
     for n, (first, count) in enumerate(PARTS):
         sl = slice(first, first + count)
         partner(isend.at[sl, :], irecv.at[sl, :], i_sem.at[n]).wait()
     both = (inner[...] + irecv[...].astype(jnp.float32)).astype(jnp.bfloat16)
     for c in chunks:
-        pm[:, column(c)] += jnp.dot(both, upv[:, column(c)], preferred_element_type=jnp.float32)
+        pm[:, column(c)] += jnp.dot(both, up_ref[:, column(c)], preferred_element_type=jnp.float32)
     last = []
     for n, (first, count) in enumerate(PARTS):
         sl = slice(first, first + count)
@@ -457,19 +453,23 @@
 
     steps = tokens // 2 // rows
     tile = PAIR * rows
-    o = pl.pallas_call(
+    o, kept = pl.pallas_call(
         attention_kernel,
-        out_shape=jax.ShapeDtypeStruct((tokens // 2, HS), bf16),
-        in_specs=[SMEM, VMEM, VMEM, VMEM],
-        out_specs=VMEM,
+        out_shape=(
+            jax.ShapeDtypeStruct((tokens // 2, HS), bf16),
+            jax.ShapeDtypeStruct(output_weight.shape, bf16),
+        ),
+        in_specs=[SMEM, VMEM, VMEM, VMEM, ANY],
+        out_specs=(VMEM, ANY),
         scratch_shapes=[
             pltpu.VMEM((pl.cdiv(tokens, BK), tile, BK), f32),
             pltpu.VMEM((tile, HS), f32),
             pltpu.VMEM((tile, 2 * HS), f32),
+            dma,
         ],
-        compiler_params=pltpu.CompilerParams(vmem_limit_bytes=40 * 2**20),
+        compiler_params=pltpu.CompilerParams(vmem_limit_bytes=24 * 2**20),
         name="attend",
-    )(request_length, qbuf, kbuf, vbuf)
+    )(request_length, qbuf, kbuf, vbuf, pltpu.with_memory_space_constraint(output_weight, pltpu.HBM))
 
     half = rows // 2
     chunks = 2 * width // COLS
@@ -477,16 +477,10 @@
     return pl.pallas_call(
         project_kernel,
         out_shape=jax.ShapeDtypeStruct((rows, 2 * width), bf16),
-        in_specs=[SMEM, SMEM] + [ANY] * 6,
+        in_specs=[SMEM, SMEM, ANY] + [VMEM] * 5,
         out_specs=ANY,
         scratch_shapes=[
             pltpu.VMEM((2, half, width), bf16),
-            pltpu.VMEM((width, 2 * width), bf16),
-            pltpu.VMEM((width, 2 * width), bf16),
-            pltpu.VMEM((rank, width), bf16),
-            pltpu.VMEM((rank, 2 * width), bf16),
-            pltpu.VMEM((half, 2 * width), bf16),
-            pltpu.VMEM((half, 2 * width), bf16),
             pltpu.VMEM((half, width), bf16),
             pltpu.VMEM((half, rank), f32),
             pltpu.VMEM((half, rank), f32),
@@ -496,14 +490,14 @@
             pltpu.VMEM((half, rank), bf16),
             pltpu.VMEM((half, rank), bf16),
             pltpu.VMEM((half, 2 * width), bf16),
-            dma((6,)), dma((parts, 2, steps)), dma((parts,)),
+            dma((parts, 2, steps)), dma((parts,)),
             dma((parts, chunks, 2)), dma((parts, 2)), dma((parts, chunks, 3)),
         ],
         compiler_params=pltpu.CompilerParams(
-            has_side_effects=True, collective_id=2, vmem_limit_bytes=48 * 2**20
+            has_side_effects=True, collective_id=2, vmem_limit_bytes=16 * 2**20
         ),
         name="project",
-    )(request_length, request_adapters, o, hidden, hbuf, output_weight, down, up)
+    )(request_length, request_adapters, o, hidden, hbuf, kept, down, up)
 
 
 def solution(mesh):

time: 102 us -> 105 us (1.029)
  Pallas kernels: 100 us -> 104 us
    pallas_call x1, Pallas kernels: 23.8 us -> 27.5 us  [local(): pl.pallas_call(attention_kernel, out_shape=(jax.ShapeDtypeStruct((tokens...]
where the time goes in v2:
time: 105 us
  Pallas kernels  104 us (99%)
    pallas_call x1, Pallas kernels, local(): pl.pallas_call(scatter_kernel, out_shape=(jax.ShapeDtypeStruct((tokens, H...  42.3 us
    pallas_call x1, Pallas kernels, local(): pl.pallas_call(project_kernel, out_shape=jax.ShapeDtypeStruct((rows, 2 *...  34.1 us
    pallas_call x1, Pallas kernels, local(): pl.pallas_call(attention_kernel, out_shape=(jax.ShapeDtypeStruct((tokens...  27.5 us

profile of v2, /device:TPU:1, one launch (start us, length us, event | category | flops | bytes accessed | tf_op | source)
XLA Modules:
  0.0 105.0 jit_solution(7254551504305407373)
XLA Ops:
  0.0 0.0 copy-start.3
  0.0 42.3 %scatter_heads.1 = (bf16[7168,128]{1,0:T(8,128)(2,1)S(1)}, bf16[7168,128]{1,0:T(8,128)(2,1)S(1)}, bf16[3584,128]{1,0:T(8,128)(2,1)S(1)}, bf16[112,2560]{1,0:T(8,128)(2,1)S(1)}) custom-call(bf16[1,224,1280]{2,1,0:T(8,128)(2,1)} %q_ref.1, bf16[1,224,1280]{2,1,0:T(8,128)(2,1)} %k_ref.1, bf16[1,224,1280]{2,1,0:T(8,128)(2,1)} %v_ref.1, bf16[1,224,2560]{2,1,0:T(8,128)(2,1)} %hid_ref.3), custom_call_target="tpu_custom_call" | custom-call | tf_op jit(solution)/shard_map/scatter_heads/pallas_call | solution.py:437
  42.3 0.0 copy-done.3
  42.3 0.0 copy-start
  42.3 0.0 copy-start.1
  42.3 0.0 copy-start.2
  42.3 0.0 copy-start.4
  42.3 27.5 %attend.1 = (bf16[3584,128]{1,0:T(8,128)(2,1)S(1)}, bf16[1280,5120]{1,0:T(8,128)(2,1)S(1)}) custom-call(s32[4]{0:T(128)S(1)} %copy-done.3, bf16[3584,128]{1,0:T(8,128)(2,1)S(1)} %get-tuple-element.11.q_ref, bf16[7168,128]{1,0:T(8,128)(2,1)S(1)} %get-tuple-element.12.k_ref, bf16[7168,128]{1,0:T(8,128)(2,1)S(1)} %get-tuple-element.13.v_ref, ...), custom_call_target="tpu_custom_call" | custom-call | tf_op jit(solution)/shard_map/attend/pallas_call | solution.py:456
  69.9 0.0 copy-done
  69.9 0.0 copy-done.1
  69.9 0.0 copy-done.2
  69.9 0.0 copy-done.4
  69.9 34.1 %project.1 = bf16[224,2560]{1,0:T(8,128)(2,1)S(1)} custom-call(s32[4]{0:T(128)S(1)} %copy-done.3, s32[4]{0:T(128)S(1)} %copy-done.4, bf16[3584,128]{1,0:T(8,128)(2,1)S(1)} %get-tuple-element.14.o_ref, bf16[1,224,2560]{2,1,0:T(8,128)(2,1)S(1)} %copy-done, bf16[112,2560]{1,0:T(8,128)(2,1)S(1)} %get-tuple-element.15.hbuf, ...), custom_call_target="tpu_custom_call" | custom-call | tf_op jit(solution)/shard_map/project/pallas_call | solution.py:477
  104.0 1.0 copy.11
Async XLA Ops:
  0.0 42.3 %copy-start.3 = (s32[4]{0:T(128)S(1)}, s32[4]{0:T(128)}, u32[]{:S(2)}) copy-start(s32[4]{0:T(128)} %len_ref.3) | copy-start | bytes 52
  42.3 27.6 %copy-start = (bf16[1,224,2560]{2,1,0:T(8,128)(2,1)S(1)}, bf16[1,224,2560]{2,1,0:T(8,128)(2,1)}, u32[]{:S(2)}) copy-start(bf16[1,224,2560]{2,1,0:T(8,128)(2,1)} %hid_ref.3) | copy-start | bytes 3440644
  42.3 27.6 %copy-start.1 = (bf16[8,32,2560]{2,1,0:T(8,128)(2,1)S(1)}, bf16[8,32,2560]{2,1,0:T(8,128)(2,1)}, u32[]{:S(2)}) copy-start(bf16[8,32,2560]{2,1,0:T(8,128)(2,1)} %param.15) | copy-start | bytes 3932164
  42.3 27.6 %copy-start.2 = (bf16[8,1280,32]{1,2,0:T(8,128)(2,1)S(1)}, bf16[8,1280,32]{1,2,0:T(8,128)(2,1)}, u32[]{:S(2)}) copy-start(bf16[8,1280,32]{1,2,0:T(8,128)(2,1)} %param.14) | copy-start | bytes 1966084
  42.3 27.6 %copy-start.4 = (s32[4]{0:T(128)S(1)}, s32[4]{0:T(128)}, u32[]{:S(2)}) copy-start(s32[4]{0:T(128)} %ad_ref.1) | copy-start | bytes 52

commit v3 on v2

--- a/solution.py
+++ b/solution.py
@@ -13,7 +13,7 @@
 GUIDE = 5.0
 BK = 1536
 PAIR = 2
-PARTS = ((0, 64), (64, 48))
+PARTS = ((0, 32), (32, 80))
 COLS = 512
 ANY = pl.BlockSpec(memory_space=pl.ANY)
 SMEM = pl.BlockSpec(memory_space=pltpu.SMEM)

time: 105 us -> 101 us (0.962)
  Pallas kernels: 104 us -> 99.3 us
    pallas_call x1, Pallas kernels: 27.5 us -> 23.8 us  [local(): pl.pallas_call(attention_kernel, out_shape=(jax.ShapeDtypeStruct((tokens...]
where the time goes in v3:
time: 101 us; the launch traced here: 100 us
  Pallas kernels  99.3 us (98%)
  local copies, waits for them, and re-layouts  1.03 us (1%)
    pallas_call x1, Pallas kernels, local(): pl.pallas_call(scatter_kernel, out_shape=(jax.ShapeDtypeStruct((tokens, H...  42.3 us
    pallas_call x1, Pallas kernels, local(): pl.pallas_call(project_kernel, out_shape=jax.ShapeDtypeStruct((rows, 2 *...  33.2 us
    pallas_call x1, Pallas kernels, local(): pl.pallas_call(attention_kernel, out_shape=(jax.ShapeDtypeStruct((tokens...  23.8 us

profile of v3, /device:TPU:1, one launch (start us, length us, event | category | flops | bytes accessed | tf_op | source)
XLA Modules:
  0.0 100.4 jit_solution(3403655776835482382)
XLA Ops:
  0.0 0.0 copy-start.3
  0.0 42.3 %scatter_heads.1 = (bf16[7168,128]{1,0:T(8,128)(2,1)S(1)}, bf16[7168,128]{1,0:T(8,128)(2,1)S(1)}, bf16[3584,128]{1,0:T(8,128)(2,1)S(1)}, bf16[112,2560]{1,0:T(8,128)(2,1)S(1)}) custom-call(bf16[1,224,1280]{2,1,0:T(8,128)(2,1)} %q_ref.1, bf16[1,224,1280]{2,1,0:T(8,128)(2,1)} %k_ref.1, bf16[1,224,1280]{2,1,0:T(8,128)(2,1)} %v_ref.1, bf16[1,224,2560]{2,1,0:T(8,128)(2,1)} %hid_ref.3), custom_call_target="tpu_custom_call" | custom-call | tf_op jit(solution)/shard_map/scatter_heads/pallas_call | solution.py:437
  42.3 0.0 copy-done.3
  42.3 0.0 copy-start
  42.3 0.0 copy-start.1
  42.3 0.0 copy-start.2
  42.3 0.0 copy-start.4
  42.3 23.8 %attend.1 = (bf16[3584,128]{1,0:T(8,128)(2,1)S(1)}, bf16[1280,5120]{1,0:T(8,128)(2,1)S(1)}) custom-call(s32[4]{0:T(128)S(1)} %copy-done.3, bf16[3584,128]{1,0:T(8,128)(2,1)S(1)} %get-tuple-element.11.q_ref, bf16[7168,128]{1,0:T(8,128)(2,1)S(1)} %get-tuple-element.12.k_ref, bf16[7168,128]{1,0:T(8,128)(2,1)S(1)} %get-tuple-element.13.v_ref, ...), custom_call_target="tpu_custom_call" | custom-call | tf_op jit(solution)/shard_map/attend/pallas_call | solution.py:456
  66.2 0.0 copy-done
  66.2 0.0 copy-done.1
  66.2 0.0 copy-done.2
  66.2 0.0 copy-done.4
  66.2 33.2 %project.1 = bf16[224,2560]{1,0:T(8,128)(2,1)S(1)} custom-call(s32[4]{0:T(128)S(1)} %copy-done.3, s32[4]{0:T(128)S(1)} %copy-done.4, bf16[3584,128]{1,0:T(8,128)(2,1)S(1)} %get-tuple-element.14.o_ref, bf16[1,224,2560]{2,1,0:T(8,128)(2,1)S(1)} %copy-done, bf16[112,2560]{1,0:T(8,128)(2,1)S(1)} %get-tuple-element.15.hbuf, ...), custom_call_target="tpu_custom_call" | custom-call | tf_op jit(solution)/shard_map/project/pallas_call | solution.py:477
  99.4 1.0 %copy.11 = bf16[224,2560]{1,0:T(8,128)(2,1)} copy(bf16[224,2560]{1,0:T(8,128)(2,1)S(1)} %project.1) | data formatting | bytes 2293760
Async XLA Ops:
  0.0 42.3 %copy-start.3 = (s32[4]{0:T(128)S(1)}, s32[4]{0:T(128)}, u32[]{:S(2)}) copy-start(s32[4]{0:T(128)} %len_ref.3) | copy-start | bytes 52
  42.3 23.9 %copy-start = (bf16[1,224,2560]{2,1,0:T(8,128)(2,1)S(1)}, bf16[1,224,2560]{2,1,0:T(8,128)(2,1)}, u32[]{:S(2)}) copy-start(bf16[1,224,2560]{2,1,0:T(8,128)(2,1)} %hid_ref.3) | copy-start | bytes 3440644
  42.3 23.9 %copy-start.1 = (bf16[8,32,2560]{2,1,0:T(8,128)(2,1)S(1)}, bf16[8,32,2560]{2,1,0:T(8,128)(2,1)}, u32[]{:S(2)}) copy-start(bf16[8,32,2560]{2,1,0:T(8,128)(2,1)} %param.15) | copy-start | bytes 3932164
  42.3 23.9 %copy-start.2 = (bf16[8,1280,32]{1,2,0:T(8,128)(2,1)S(1)}, bf16[8,1280,32]{1,2,0:T(8,128)(2,1)}, u32[]{:S(2)}) copy-start(bf16[8,1280,32]{1,2,0:T(8,128)(2,1)} %param.14) | copy-start | bytes 1966084
  42.3 23.9 %copy-start.4 = (s32[4]{0:T(128)S(1)}, s32[4]{0:T(128)}, u32[]{:S(2)}) copy-start(s32[4]{0:T(128)} %ad_ref.1) | copy-start | bytes 52

commit v4 on v3

--- a/solution.py
+++ b/solution.py
@@ -11,7 +11,7 @@
 MESH = pl.DeviceIdType.MESH
 HS = 128
 GUIDE = 5.0
-BK = 1536
+BK = 2304
 PAIR = 2
 PARTS = ((0, 32), (32, 80))
 COLS = 512
@@ -193,69 +193,76 @@
             lo = jnp.where(seg_first == n, starts[n], lo)
             hi = jnp.where(seg_last == n, ends[n], hi)
         base = (lo // 32) * 32
-        blocks = pl.cdiv(hi - base, BK)
+        rest = (hi - base) % BK
+        large = (hi - base) // BK + jnp.where(rest > BK // 2, 1, 0)
+        small = jnp.where(jnp.logical_and(rest > 0, rest <= BK // 2), 1, 0)
         single = seg_first == seg_last
         row = lax.broadcasted_iota(jnp.int32, (rows, 1), 0)
         seg_q = segment(first + row + (row // piece) * piece)
         m_ref[...] = jnp.full_like(m_ref, -1e30)
 
-        def widest(x):
-            out = m_ref[...]
-            for n in range(BK // HS):
-                out = jnp.maximum(out, x[:, n * HS : (n + 1) * HS])
-            m_ref[...] = out
-
-        def scores(at):
-            return lax.dot_general(
-                q_ref[own, :], k_ref[pl.ds(at, BK), :], (((1,), (1,)), ((), ())),
-                preferred_element_type=jnp.float32,
+        def scores(n, size):
+            logical = base + n * BK
+            at = pl.multiple_of(jnp.minimum(logical, tokens - size), 32)
+            whole = jnp.logical_and(
+                single, jnp.logical_and(logical >= lo, logical + size <= hi)
             )
 
-        @pl.loop(0, blocks)
-        def _(n):
-            logical = base + n * BK
-            at = pl.multiple_of(jnp.minimum(logical, tokens - BK), 32)
-            whole = jnp.logical_and(
-                single, jnp.logical_and(logical >= lo, logical + BK <= hi)
-            )
+            def product():
+                return lax.dot_general(
+                    q_ref[own, :], k_ref[pl.ds(at, size), :], (((1,), (1,)), ((), ())),
+                    preferred_element_type=jnp.float32,
+                )
+
+            def keep(score):
+                s_ref[n, :, :size] = score
+                widest = m_ref[...]
+                for j in range(size // HS):
+                    widest = jnp.maximum(widest, score[:, j * HS : (j + 1) * HS])
+                m_ref[...] = widest
 
             @pl.when(whole)
             def _():
-                score = scores(at)
-                s_ref[n] = score
-                widest(score)
+                keep(product())
 
             @pl.when(jnp.logical_not(whole))
             def _():
-                pos = at + lax.broadcasted_iota(jnp.int32, (1, BK), 1)
+                pos = at + lax.broadcasted_iota(jnp.int32, (1, size), 1)
                 seg_k = jnp.where(pos >= logical, segment(pos), -1)
-                score = jnp.where(seg_q == seg_k, scores(at), -jnp.inf)
-                s_ref[n] = score
-                widest(score)
-
-        m_ref[...] = jnp.broadcast_to(
-            jnp.max(m_ref[...], axis=1, keepdims=True), m_ref.shape
-        )
-        acc_ref[...] = jnp.zeros_like(acc_ref)
-
-        @pl.loop(0, blocks)
-        def _(n):
-            at = pl.multiple_of(jnp.minimum(base + n * BK, tokens - BK), 32)
+                keep(jnp.where(seg_q == seg_k, product(), -jnp.inf))
+
+        def weigh(n, size):
+            at = pl.multiple_of(jnp.minimum(base + n * BK, tokens - size), 32)
             top = m_ref[...]
             weight = jnp.concatenate(
                 [
                     jnp.exp2((s_ref[n, :, j * HS : (j + 1) * HS] - top) * factor).astype(
                         jnp.bfloat16
                     )
-                    for j in range(BK // HS)
+                    for j in range(size // HS)
                 ],
                 axis=1,
             )
             values = jnp.concatenate(
-                [v_ref[pl.ds(at, BK), :], jnp.ones((BK, HS), jnp.bfloat16)], axis=1
+                [v_ref[pl.ds(at, size), :], jnp.ones((size, HS), jnp.bfloat16)], axis=1
             )
             acc_ref[...] += jnp.dot(weight, values, preferred_element_type=jnp.float32)
 
+        def over_blocks(work):
+            @pl.loop(0, large)
+            def _(n):
+                work(n, BK)
+
+            @pl.loop(large, large + small)
+            def _(n):
+                work(n, BK // 2)
+
+        over_blocks(scores)
+        m_ref[...] = jnp.broadcast_to(
+            jnp.max(m_ref[...], axis=1, keepdims=True), m_ref.shape
+        )
+        acc_ref[...] = jnp.zeros_like(acc_ref)
+        over_blocks(weigh)
         o_ref[own, :] = (acc_ref[:, :HS] / acc_ref[:, HS:]).astype(o_ref.dtype)
 
     fetch.wait()

time: 101 us -> 102 us (level)
  Pallas kernels: 99.3 us -> 101 us
    pallas_call x1, Pallas kernels: 23.8 us -> 25.6 us  [local(): pl.pallas_call(attention_kernel, out_shape=(jax.ShapeDtypeStruct((tokens...]
where the time goes in v4:
time: 102 us
  Pallas kernels  101 us (99%)
  local copies, waits for them, and re-layouts  1.03 us (1%)
    pallas_call x1, Pallas kernels, local(): pl.pallas_call(scatter_kernel, out_shape=(jax.ShapeDtypeStruct((tokens, H...  42.3 us
    pallas_call x1, Pallas kernels, local(): pl.pallas_call(project_kernel, out_shape=jax.ShapeDtypeStruct((rows, 2 *...  33 us
    pallas_call x1, Pallas kernels, local(): pl.pallas_call(attention_kernel, out_shape=(jax.ShapeDtypeStruct((tokens...  25.6 us

profile of v4, /device:TPU:1, one launch (start us, length us, event | category | flops | bytes accessed | tf_op | source)
XLA Modules:
  0.0 102.0 jit_solution(3663434634154822742)
XLA Ops:
  0.0 0.0 copy-start.3
  0.0 42.3 %scatter_heads.1 = (bf16[7168,128]{1,0:T(8,128)(2,1)S(1)}, bf16[7168,128]{1,0:T(8,128)(2,1)S(1)}, bf16[3584,128]{1,0:T(8,128)(2,1)S(1)}, bf16[112,2560]{1,0:T(8,128)(2,1)S(1)}) custom-call(bf16[1,224,1280]{2,1,0:T(8,128)(2,1)} %q_ref.1, bf16[1,224,1280]{2,1,0:T(8,128)(2,1)} %k_ref.1, bf16[1,224,1280]{2,1,0:T(8,128)(2,1)} %v_ref.1, bf16[1,224,2560]{2,1,0:T(8,128)(2,1)} %hid_ref.3), custom_call_target="tpu_custom_call" | custom-call | tf_op jit(solution)/shard_map/scatter_heads/pallas_call | solution.py:444
  42.3 0.0 copy-done.3
  42.3 0.0 copy-start
  42.3 0.0 copy-start.1
  42.3 0.0 copy-start.2
  42.3 0.0 copy-start.4
  42.3 25.6 %attend.1 = (bf16[3584,128]{1,0:T(8,128)(2,1)S(1)}, bf16[1280,5120]{1,0:T(8,128)(2,1)S(1)}) custom-call(s32[4]{0:T(128)S(1)} %copy-done.3, bf16[3584,128]{1,0:T(8,128)(2,1)S(1)} %get-tuple-element.11.q_ref, bf16[7168,128]{1,0:T(8,128)(2,1)S(1)} %get-tuple-element.12.k_ref, bf16[7168,128]{1,0:T(8,128)(2,1)S(1)} %get-tuple-element.13.v_ref, ...), custom_call_target="tpu_custom_call" | custom-call | tf_op jit(solution)/shard_map/attend/pallas_call | solution.py:463
  68.0 0.0 copy-done
  68.0 0.0 copy-done.1
  68.0 0.0 copy-done.2
  68.0 0.0 copy-done.4
  68.0 33.0 %project.1 = bf16[224,2560]{1,0:T(8,128)(2,1)S(1)} custom-call(s32[4]{0:T(128)S(1)} %copy-done.3, s32[4]{0:T(128)S(1)} %copy-done.4, bf16[3584,128]{1,0:T(8,128)(2,1)S(1)} %get-tuple-element.14.o_ref, bf16[1,224,2560]{2,1,0:T(8,128)(2,1)S(1)} %copy-done, bf16[112,2560]{1,0:T(8,128)(2,1)S(1)} %get-tuple-element.15.hbuf, ...), custom_call_target="tpu_custom_call" | custom-call | tf_op jit(solution)/shard_map/project/pallas_call | solution.py:484
  101.0 1.0 copy.11
Async XLA Ops:
  0.0 42.3 %copy-start.3 = (s32[4]{0:T(128)S(1)}, s32[4]{0:T(128)}, u32[]{:S(2)}) copy-start(s32[4]{0:T(128)} %len_ref.3) | copy-start | bytes 52
  42.3 25.7 %copy-start = (bf16[1,224,2560]{2,1,0:T(8,128)(2,1)S(1)}, bf16[1,224,2560]{2,1,0:T(8,128)(2,1)}, u32[]{:S(2)}) copy-start(bf16[1,224,2560]{2,1,0:T(8,128)(2,1)} %hid_ref.3) | copy-start | bytes 3440644
  42.3 25.7 %copy-start.1 = (bf16[8,32,2560]{2,1,0:T(8,128)(2,1)S(1)}, bf16[8,32,2560]{2,1,0:T(8,128)(2,1)}, u32[]{:S(2)}) copy-start(bf16[8,32,2560]{2,1,0:T(8,128)(2,1)} %param.15) | copy-start | bytes 3932164
  42.3 25.7 %copy-start.2 = (bf16[8,1280,32]{1,2,0:T(8,128)(2,1)S(1)}, bf16[8,1280,32]{1,2,0:T(8,128)(2,1)}, u32[]{:S(2)}) copy-start(bf16[8,1280,32]{1,2,0:T(8,128)(2,1)} %param.14) | copy-start | bytes 1966084
  42.3 25.7 %copy-start.4 = (s32[4]{0:T(128)S(1)}, s32[4]{0:T(128)}, u32[]{:S(2)}) copy-start(s32[4]{0:T(128)} %ad_ref.1) | copy-start | bytes 52

commit v5 on v4

--- a/solution.py
+++ b/solution.py
@@ -331,7 +331,7 @@
             @pl.loop(0, blocks)
             def _(i):
                 for core in range(2):
-                    send_o((i + s // 2) % blocks, n, core, True)
+                    send_o(i, n, core, True)
 
     def partner(src, dst, sems):
         return pltpu.make_async_remote_copy(

time: 102 us -> 98 us (0.961); the launches traced: 102 us -> 96.9 us
  Pallas kernels: 101 us -> 95.8 us
    pallas_call x1, Pallas kernels: 25.6 us -> 21.5 us  [local(): pl.pallas_call(attention_kernel, out_shape=(jax.ShapeDtypeStruct((tokens...]
where the time goes in v5:
time: 98 us; the launch traced here: 96.9 us
  Pallas kernels  95.8 us (98%)
  local copies, waits for them, and re-layouts  1.03 us (1%)
    pallas_call x1, Pallas kernels, local(): pl.pallas_call(scatter_kernel, out_shape=(jax.ShapeDtypeStruct((tokens, H...  42.3 us
    pallas_call x1, Pallas kernels, local(): pl.pallas_call(project_kernel, out_shape=jax.ShapeDtypeStruct((rows, 2 *...  32 us
    pallas_call x1, Pallas kernels, local(): pl.pallas_call(attention_kernel, out_shape=(jax.ShapeDtypeStruct((tokens...  21.5 us

profile of v5, /device:TPU:1, one launch (start us, length us, event | category | flops | bytes accessed | tf_op | source)
XLA Modules:
  0.0 96.9 jit_solution(13959146492886663540)
XLA Ops:
  0.0 0.0 copy-start.3
  0.0 42.3 %scatter_heads.1 = (bf16[7168,128]{1,0:T(8,128)(2,1)S(1)}, bf16[7168,128]{1,0:T(8,128)(2,1)S(1)}, bf16[3584,128]{1,0:T(8,128)(2,1)S(1)}, bf16[112,2560]{1,0:T(8,128)(2,1)S(1)}) custom-call(bf16[1,224,1280]{2,1,0:T(8,128)(2,1)} %q_ref.1, bf16[1,224,1280]{2,1,0:T(8,128)(2,1)} %k_ref.1, bf16[1,224,1280]{2,1,0:T(8,128)(2,1)} %v_ref.1, bf16[1,224,2560]{2,1,0:T(8,128)(2,1)} %hid_ref.3), custom_call_target="tpu_custom_call" | custom-call | tf_op jit(solution)/shard_map/scatter_heads/pallas_call | solution.py:444
  42.3 0.0 copy-done.3
  42.3 0.0 copy-start
  42.3 0.0 copy-start.1
  42.3 0.0 copy-start.2
  42.3 0.0 copy-start.4
  42.3 21.5 %attend.1 = (bf16[3584,128]{1,0:T(8,128)(2,1)S(1)}, bf16[1280,5120]{1,0:T(8,128)(2,1)S(1)}) custom-call(s32[4]{0:T(128)S(1)} %copy-done.3, bf16[3584,128]{1,0:T(8,128)(2,1)S(1)} %get-tuple-element.11.q_ref, bf16[7168,128]{1,0:T(8,128)(2,1)S(1)} %get-tuple-element.12.k_ref, bf16[7168,128]{1,0:T(8,128)(2,1)S(1)} %get-tuple-element.13.v_ref, ...), custom_call_target="tpu_custom_call" | custom-call | tf_op jit(solution)/shard_map/attend/pallas_call | solution.py:463
  63.8 0.0 copy-done
  63.9 0.0 copy-done.1
  63.9 0.0 copy-done.2
  63.9 0.0 copy-done.4
  63.9 32.0 %project.1 = bf16[224,2560]{1,0:T(8,128)(2,1)S(1)} custom-call(s32[4]{0:T(128)S(1)} %copy-done.3, s32[4]{0:T(128)S(1)} %copy-done.4, bf16[3584,128]{1,0:T(8,128)(2,1)S(1)} %get-tuple-element.14.o_ref, bf16[1,224,2560]{2,1,0:T(8,128)(2,1)S(1)} %copy-done, bf16[112,2560]{1,0:T(8,128)(2,1)S(1)} %get-tuple-element.15.hbuf, ...), custom_call_target="tpu_custom_call" | custom-call | tf_op jit(solution)/shard_map/project/pallas_call | solution.py:484
  95.9 1.0 %copy.11 = bf16[224,2560]{1,0:T(8,128)(2,1)} copy(bf16[224,2560]{1,0:T(8,128)(2,1)S(1)} %project.1) | data formatting | bytes 2293760
Async XLA Ops:
  0.0 42.3 %copy-start.3 = (s32[4]{0:T(128)S(1)}, s32[4]{0:T(128)}, u32[]{:S(2)}) copy-start(s32[4]{0:T(128)} %len_ref.3) | copy-start | bytes 52
  42.3 21.6 %copy-start = (bf16[1,224,2560]{2,1,0:T(8,128)(2,1)S(1)}, bf16[1,224,2560]{2,1,0:T(8,128)(2,1)}, u32[]{:S(2)}) copy-start(bf16[1,224,2560]{2,1,0:T(8,128)(2,1)} %hid_ref.3) | copy-start | bytes 3440644
  42.3 21.6 %copy-start.1 = (bf16[8,32,2560]{2,1,0:T(8,128)(2,1)S(1)}, bf16[8,32,2560]{2,1,0:T(8,128)(2,1)}, u32[]{:S(2)}) copy-start(bf16[8,32,2560]{2,1,0:T(8,128)(2,1)} %param.15) | copy-start | bytes 3932164
  42.3 21.6 %copy-start.2 = (bf16[8,1280,32]{1,2,0:T(8,128)(2,1)S(1)}, bf16[8,1280,32]{1,2,0:T(8,128)(2,1)}, u32[]{:S(2)}) copy-start(bf16[8,1280,32]{1,2,0:T(8,128)(2,1)} %param.14) | copy-start | bytes 1966084
  42.3 21.6 %copy-start.4 = (s32[4]{0:T(128)S(1)}, s32[4]{0:T(128)}, u32[]{:S(2)}) copy-start(s32[4]{0:T(128)} %ad_ref.1) | copy-start | bytes 52
